TPU v7x, 256 devices: a whole 4x4x8 slice. The times are simulated.
256 devices in a mesh: cluster: 8 (over y, core), sub: 32 (over z, x).
Axes of the slice: x: 4, y: 4, z: 8, core: 2. Of those that a mesh axis runs over, the one named last changes fastest.
Arguments:
- dual_ops: float32 [8, 32, 1536, 1536], P('cluster', 'sub')
- rhs: float32 [8, 32, 1536, 128], P('cluster', 'sub'), may hold values from -6 to 6
- corner_basis: float32 [8, 32, 24, 1536], P('cluster', 'sub'), may hold values from -0.15625 to 0.15625
- scaling: float32 [8, 32, 1536], P('cluster', 'sub'), may hold values from 0.5 to 1.5
- cluster_corner_inverse: float32 [8, 384, 384], P('cluster'), may hold values from -0.3125 to 0.3125
- coarse_map: float32 [8, 48, 384], P('cluster'), may hold values from -0.3125 to 0.3125
- global_inv: float32 [48, 48], replicated, may hold values from -0.875 to 0.875
- row_index: int32 [8, 32, 4, 384], P('cluster', 'sub'), may hold values from 0 to 1535, as said below
- pair_counts: int32 [8, 32, 4], P('cluster', 'sub'), may hold values from 0 to 384, as said below
- corner_map: int32 [8, 32, 24], P('cluster', 'sub'), may hold values from 0 to 383
Outputs:
- multipliers: float32 [8, 32, 1536, 128], P('cluster', 'sub')
- residual: float32 [8, 32, 1536, 128], P('cluster', 'sub')
Inputs may be any that keep to these rules, and one draw needn't show every extreme that they name: `row_index`: the 384 entries of one subdomain's four directions together hold every row 0 to 1535 once. pair_counts of a direction equals the neighbour's count of the direction pointing back; it is 0 toward a missing neighbour.
All inputs are finite; a program needn't handle non-finite values.
Results may differ from a plain program's by a relative error of at most 0.00027.
Values sent between devices are 32-bit elements; how exact they have to be, the bound alone decides.
No kernel may reach another device: no remote copies, remote signals or barrier semaphores. Data moves between devices by JAX's collectives and lax.ppermute only.
A program may use at most 64 MiB of HBM per device.

v0:
```python
import jax
import jax.numpy as jnp
from jax import lax
from jax.sharding import PartitionSpec as P

ITERS = 3


HIGHEST_ACCURACY = lax.Precision.HIGHEST


def with_halo(block, sides, width):
    for axis, dim in sides:
        count = lax.axis_size(axis)
        forward = [(i, i + 1) for i in range(count - 1)]
        backward = [(target, source) for source, target in forward]
        low = lax.ppermute(
            lax.slice_in_dim(block, block.shape[dim] - width, None, axis=dim), axis, forward
        )
        high = lax.ppermute(lax.slice_in_dim(block, 0, width, axis=dim), axis, backward)
        block = jnp.concatenate([low, block, high], axis=dim)
    return block


def product(left, right):
    return jnp.dot(left, right, precision=HIGHEST_ACCURACY, preferred_element_type=jnp.float32)


def body(
    dual_ops,
    rhs,
    corner_basis,
    scaling,
    cluster_corner_inverse,
    coarse_map,
    global_inv,
    row_index,
    pair_counts,
    corner_map,
):
    operator = dual_ops[0, 0]
    loads = rhs[0, 0]
    basis = corner_basis[0, 0]
    weights = scaling[0, 0]
    cluster_factor = cluster_corner_inverse[0]
    lift_map = coarse_map[0]
    row_ids = row_index[0, 0]
    counts = pair_counts[0, 0]
    corners = corner_map[0, 0]
    slot_len = row_ids.shape[1]
    order = operator.shape[0]
    coarse_len = cluster_factor.shape[0]
    live_slot = (jnp.arange(slot_len, dtype=jnp.int32)[None, :] < counts[:, None]).astype(
        jnp.float32
    )
    flat_ids = row_ids.reshape(-1)
    live_rows = jnp.zeros((order,), jnp.float32).at[flat_ids].add(live_slot.reshape(-1))
    onehot = (corners[:, None] == jnp.arange(coarse_len, dtype=jnp.int32)[None, :]).astype(
        jnp.float32
    )

    def jump(vector):
        slot_vals = vector[row_ids] * live_slot[:, :, None]
        sub_ext = with_halo(
            jnp.concatenate([slot_vals[0], slot_vals[1]], 0), (("sub", 0),), slot_len
        )
        cluster_extension = with_halo(
            jnp.concatenate([slot_vals[2], slot_vals[3]], 0), (("cluster", 0),), slot_len
        )
        received = jnp.stack(
            [
                sub_ext[:slot_len],
                sub_ext[3 * slot_len :],
                cluster_extension[:slot_len],
                cluster_extension[3 * slot_len :],
            ],
            0,
        )
        received = received * live_slot[:, :, None]
        returned = jnp.zeros_like(vector).at[flat_ids].add(received.reshape(-1, vector.shape[1]))
        return live_rows[:, None] * (vector - returned)

    def precondition(vector):
        corner_local = product(basis, vector)
        partial_res = product(onehot.T, corner_local)
        corner_residual = lax.psum(partial_res, "sub")
        halfway_solution = product(cluster_factor, corner_residual)
        coarse_solution = product(cluster_factor.T, halfway_solution)
        global_res = lax.psum(product(lift_map, corner_residual), "cluster")
        global_half = product(global_inv, global_res)
        global_x = product(global_inv.T, global_half)
        cluster_vec = coarse_solution + product(lift_map.T, global_x)
        corner_vals = product(onehot, cluster_vec)
        scaled = weights[:, None] * vector + product(basis.T, corner_vals)
        precond = jump(scaled)
        residual_product_value = lax.psum(jnp.sum(vector * precond, axis=0), ("cluster", "sub"))
        return (precond, residual_product_value)

    multipliers = jnp.zeros_like(loads)
    residual = jump(loads)
    precond, rz_now = precondition(residual)
    search = precond
    for step in range(ITERS):
        image = jump(product(operator, search))
        alpha = rz_now / lax.psum(jnp.sum(search * image, axis=0), ("cluster", "sub"))
        multipliers = multipliers + alpha * search
        residual = residual - alpha * image
        precond, rz_next = precondition(residual)
        search = precond + rz_next / rz_now * search
        rz_now = rz_next
    return (multipliers[None, None], residual[None, None])


def solution(mesh):
    in_specs = (
        P("cluster", "sub", None, None),
        P("cluster", "sub", None, None),
        P("cluster", "sub", None, None),
        P("cluster", "sub", None),
        P("cluster", None, None),
        P("cluster", None, None),
        P(),
        P("cluster", "sub", None, None),
        P("cluster", "sub", None),
        P("cluster", "sub", None),
    )
    out_specs = (P("cluster", "sub", None, None), P("cluster", "sub", None, None))
    return jax.shard_map(body, mesh=mesh, in_specs=in_specs, out_specs=out_specs, check_vma=False)
```

profile of v0, /device:TPU:8, one launch (start us, length us, event | category | flops | bytes accessed | tf_op | source)
XLA Modules:
  0.0 1237.4 jit_solution(15961390772995018659)
XLA Ops:
  8.8 3.8 gather_fusion
  13.7 3.4 collective-permute-start
  19.1 2.4 collective-permute-start.2
  23.1 8.7 scatter_custom_fusion
  32.3 8.9 scatter_custom_fusion.1
  43.5 147.8 %all-reduce.5.cloned.1.call-done = f32[384,128]{1,0:T(8,128)} async-done(((f32[384,128]{1,0:T(8,128)}), f32[384,128]{1,0:T(8,128)}) %all-reduce.5.cloned.1.call-update) | async-done | bytes 196624 | tf_op jit(solution)/shard_map/psum | solution.py:86
  195.0 21.0 %psum.85 = f32[48,128]{0,1:T(8,128)S(1)} all-reduce(f32[48,128]{0,1:T(8,128)S(1)} %convolution_bitcast_fusion.5), channel_id=1, replica_groups=mesh['cluster'=8,'sub'=32] {'cluster'}, use_global_device_ids=true, to_apply=%region_3.0 | all-reduce | flops 6144 | bytes 49152 | tf_op jit(solution)/shard_map/psum | solution.py:89
  218.1 3.7 gather_fusion.1
  231.3 4.9 collective-permute-done.6
  239.7 9.3 scatter_custom_fusion.2
  251.4 13.3 %fusion.9 = f32[1536,128]{0,1:T(8,128)} fusion(f32[1536,128]{0,1:T(8,128)S(1)} %subtract_multiply_fusion.5, f32[1,1,1536,1536]{3,2,1,0:T(8,128)} %param.10), kind=kOutput, calls=%fused_computation.27 | convolution fusion | flops 3623878656 | bytes 11010048 | tf_op jit(solution)/shard_map/dot_general | solution.py:26
  266.1 3.7 gather_fusion.2
  271.4 3.1 collective-permute-start.8
  274.5 3.9 collective-permute-start.11
  281.7 3.7 collective-permute-done.10
  285.4 2.5 collective-permute-done.9
  289.1 10.0 scatter_custom_fusion.3
  303.1 83.1 %all-reduce = (f32[128]{0:T(128)S(1)}, f32[128]{0:T(128)S(1)}) all-reduce(f32[128]{0:T(128)S(1)} %get-tuple-element.7, f32[128]{0:T(128)S(1)} %get-tuple-element.6), channel_id=1, replica_groups=mesh['cluster'=8,'sub'=32] {'cluster','sub'}, use_global_device_ids=true, to_apply=%region_6.0 | all-reduce | flops 256 | bytes 2048 | tf_op jit(solution)/shard_map/psum | solution.py:96
  389.7 138.9 %all-reduce.7.cloned.1.call-done = f32[384,128]{1,0:T(8,128)} async-done(((f32[384,128]{1,0:T(8,128)}), f32[384,128]{1,0:T(8,128)}) %all-reduce.7.cloned.1.call-update) | async-done | bytes 196624 | tf_op jit(solution)/shard_map/psum | solution.py:86
  532.4 21.0 %psum.89 = f32[48,128]{0,1:T(8,128)S(1)} all-reduce(f32[48,128]{0,1:T(8,128)S(1)} %convolution_bitcast_fusion.4), channel_id=1, replica_groups=mesh['cluster'=8,'sub'=32] {'cluster'}, use_global_device_ids=true, to_apply=%region_11.0 | all-reduce | flops 6144 | bytes 49152 | tf_op jit(solution)/shard_map/psum | solution.py:89
  556.3 3.7 gather_fusion.3
  569.4 5.1 collective-permute-done.14
  578.0 10.0 scatter_custom_fusion.4
  591.9 80.7 %psum.90 = f32[128]{0:T(128)S(1)} all-reduce(f32[128]{0:T(128)S(1)} %multiply_reduce_fusion.3), channel_id=1, replica_groups=mesh['cluster'=8,'sub'=32] {'cluster','sub'}, use_global_device_ids=true, to_apply=%region_14.0 | all-reduce | flops 128 | bytes 1024 | tf_op jit(solution)/shard_map/psum | solution.py:96
  674.8 13.0 %fusion.12 = f32[1536,128]{0,1:T(8,128)} fusion(f32[1536,128]{0,1:T(8,128)S(1)} %multiply_add_fusion.1, f32[1,1,1536,1536]{3,2,1,0:T(8,128)} %param.10), kind=kOutput, calls=%fused_computation.28 | convolution fusion | flops 3623878656 | bytes 11010048 | tf_op jit(solution)/shard_map/dot_general | solution.py:26
  689.3 3.7 gather_fusion.4
  695.9 3.7 collective-permute-start.19
  702.8 3.7 collective-permute-done.18
  706.6 4.2 collective-permute-done.17
  712.0 10.0 scatter_custom_fusion.5
  722.0 2.3 copy.48
  725.9 79.0 %psum.91 = f32[128]{0:T(128)S(1)} all-reduce(f32[128]{0:T(128)S(1)} %multiply_reduce_fusion.2), channel_id=1, replica_groups=mesh['cluster'=8,'sub'=32] {'cluster','sub'}, use_global_device_ids=true, to_apply=%region_17.0 | all-reduce | flops 128 | bytes 1024 | tf_op jit(solution)/shard_map/psum | solution.py:105
  808.0 139.4 %all-reduce.9.cloned.1.call-done = f32[384,128]{1,0:T(8,128)} async-done(((f32[384,128]{1,0:T(8,128)}), f32[384,128]{1,0:T(8,128)}) %all-reduce.9.cloned.1.call-update) | async-done | bytes 196624 | tf_op jit(solution)/shard_map/psum | solution.py:86
  951.1 21.2 %psum.93 = f32[48,128]{0,1:T(8,128)S(1)} all-reduce(f32[48,128]{0,1:T(8,128)S(1)} %convolution_bitcast_fusion.3), channel_id=1, replica_groups=mesh['cluster'=8,'sub'=32] {'cluster'}, use_global_device_ids=true, to_apply=%region_19.0 | all-reduce | flops 6144 | bytes 49152 | tf_op jit(solution)/shard_map/psum | solution.py:89
  975.3 3.7 gather_fusion.5
  988.3 5.1 collective-permute-done.22
  996.9 10.0 scatter_custom_fusion.6
  1006.9 2.3 copy.50
  1010.8 80.6 %psum.94 = f32[128]{0:T(128)S(1)} all-reduce(f32[128]{0:T(128)S(1)} %multiply_reduce_fusion.1), channel_id=1, replica_groups=mesh['cluster'=8,'sub'=32] {'cluster','sub'}, use_global_device_ids=true, to_apply=%region_22.0 | all-reduce | flops 128 | bytes 1024 | tf_op jit(solution)/shard_map/psum | solution.py:96
  1093.6 12.2 fusion.15
  1107.0 3.7 gather_fusion.6
  1113.5 3.7 collective-permute-start.27
  1120.8 3.5 collective-permute-done.26
  1124.2 4.2 collective-permute-done.25
  1129.6 10.0 scatter_custom_fusion.7
  1139.6 2.3 copy.52
  1143.7 79.0 %psum.95 = f32[128]{0:T(128)S(1)} all-reduce(f32[128]{0:T(128)S(1)} %multiply_reduce_fusion), channel_id=1, replica_groups=mesh['cluster'=8,'sub'=32] {'cluster','sub'}, use_global_device_ids=true, to_apply=%region_25.0 | all-reduce | flops 128 | bytes 1024 | tf_op jit(solution)/shard_map/psum | solution.py:105
  1222.7 3.2 subtract_bitcast_fusion
  (188 shorter events, 121.8 us)
Async XLA Ops:
  7.2 184.1 %copy-start = (f32[1,384,384]{2,1,0:T(8,128)S(1)}, f32[1,384,384]{2,1,0:T(8,128)}, u32[]{:S(2)}) copy-start(f32[1,384,384]{2,1,0:T(8,128)} %param.14) | copy-start | bytes 1769476
  7.2 15.6 %copy-start.1 = (f32[1,1,1536,128]{3,2,1,0:T(8,128)S(1)}, f32[1,1,1536,128]{3,2,1,0:T(8,128)}, u32[]{:S(2)}) copy-start(f32[1,1,1536,128]{3,2,1,0:T(8,128)} %param.11) | copy-start | bytes 2359300
  7.2 184.1 %all-reduce.5.cloned.1.call-start = ((), (), s32[]{:S(2)}) async-start(), calls=%async_computation | async-start | bytes 393216 | tf_op jit(solution)/shard_map/psum | solution.py:86
  8.8 32.8 %copy-start.17 = (f32[1,1,24,1536]{3,2,1,0:T(8,128)S(1)}, f32[1,1,24,1536]{3,2,1,0:T(8,128)}, u32[]{:S(2)}) copy-start(f32[1,1,24,1536]{3,2,1,0:T(8,128)} %param.12) | copy-start | bytes 442372
  8.8 33.6 %copy-start.21 = (s32[1,1,24]{2,1,0:T(1,128)S(1)}, s32[1,1,24]{2,1,0:T(1,128)}, u32[]{:S(2)}) copy-start(s32[1,1,24]{2,1,0:T(1,128)} %param.19) | copy-start | bytes 292
  8.8 34.7 %copy-start.22 = (f32[1,1,1536]{2,1,0:T(1,128)S(1)}, f32[1,1,1536]{2,1,0:T(1,128)}, u32[]{:S(2)}) copy-start(f32[1,1,1536]{2,1,0:T(1,128)} %param.13) | copy-start | bytes 18436
  12.6 181.0 %copy-start.18 = (f32[1,48,384]{2,1,0:T(8,128)S(1)}, f32[1,48,384]{2,1,0:T(8,128)}, u32[]{:S(2)}) copy-start(f32[1,48,384]{2,1,0:T(8,128)} %param.15) | copy-start | bytes 221188
  12.6 203.4 %copy-start.19 = (f32[48,48]{1,0:T(8,128)S(1)}, f32[48,48]{1,0:T(8,128)}, u32[]{:S(2)}) copy-start(f32[48,48]{1,0:T(8,128)} %param.16) | copy-start | bytes 27652
  13.7 18.2 %collective-permute-start = (f32[384,128]{1,0:T(8,128)}, f32[384,128]{1,0:T(8,128)S(1)}, u32[]{:S(2)}, u32[]{:S(2)}) collective-permute-start(f32[384,128]{1,0:T(8,128)} %get-tuple-element.34), channel_id=1, source_target_pairs={{0,1},{1,2},{2,3},{3,4},{4,5},{5,6},{6,7},{7,8},{8,9},{9,10},{10,1... | collective-permute-start | bytes 589832 | tf_op jit(solution)/shard_map/ppermute | solution.py:17
  17.1 14.8 %collective-permute-start.3 = (f32[384,128]{1,0:T(8,128)}, f32[384,128]{1,0:T(8,128)S(1)}, u32[]{:S(2)}, u32[]{:S(2)}) collective-permute-start(f32[384,128]{1,0:T(8,128)} %get-tuple-element.35), channel_id=1, source_target_pairs={{32,0},{64,32},{96,64},{128,96},{160,128},{192,160},{224,192},{33,... | collective-permute-start | bytes 589832 | tf_op jit(solution)/shard_map/ppermute | solution.py:20
  19.1 12.8 %collective-permute-start.2 = (f32[384,128]{1,0:T(8,128)}, f32[384,128]{1,0:T(8,128)S(1)}, u32[]{:S(2)}, u32[]{:S(2)}) collective-permute-start(f32[384,128]{1,0:T(8,128)} %get-tuple-element.36), channel_id=1, source_target_pairs={{0,32},{32,64},{64,96},{96,128},{128,160},{160,192},{192,224},{1,3... | collective-permute-start | bytes 589832 | tf_op jit(solution)/shard_map/ppermute | solution.py:17
  21.5 10.4 collective-permute-start.1
  43.4 485.2 %all-reduce.7.cloned.1.call-start = ((), (), s32[]{:S(2)}) async-start(), calls=%async_computation.1 | async-start | bytes 393216 | tf_op jit(solution)/shard_map/psum | solution.py:86
  223.3 8.0 collective-permute-start.4
  225.5 5.9 collective-permute-start.7
  227.5 8.7 collective-permute-start.6
  229.8 8.7 collective-permute-start.5
  251.4 50.0 %copy-start.2 = (f32[1536,128]{0,1:T(8,128)}, f32[1536,128]{0,1:T(8,128)S(1)}, u32[]{:S(2)}) copy-start(f32[1536,128]{0,1:T(8,128)S(1)} %subtract_multiply_fusion.5) | copy-start | bytes 2359300
  269.8 116.3 %copy-start.13 = (f32[1536,128]{0,1:T(8,128)S(1)}, f32[1536,128]{0,1:T(8,128)}, u32[]{:S(2)}) copy-start(f32[1536,128]{0,1:T(8,128)} %fusion.9) | copy-start | bytes 2359300
  271.4 10.3 collective-permute-start.8
  274.5 7.2 collective-permute-start.11
  278.4 7.0 collective-permute-start.10
  280.4 7.6 collective-permute-start.9
  389.2 558.1 %all-reduce.9.cloned.1.call-start = ((), (), s32[]{:S(2)}) async-start(), calls=%async_computation.2 | async-start | bytes 393216 | tf_op jit(solution)/shard_map/psum | solution.py:86
  556.3 116.3 %copy-start.3 = (f32[1536,128]{0,1:T(8,128)S(1)}, f32[1536,128]{0,1:T(8,128)}, u32[]{:S(2)}) copy-start(f32[1536,128]{0,1:T(8,128)} %copy-done.2) | copy-start | bytes 2359300
  560.0 112.6 %copy-start.12 = (f32[1536,128]{0,1:T(8,128)S(1)}, f32[1536,128]{0,1:T(8,128)}, u32[]{:S(2)}) copy-start(f32[1536,128]{0,1:T(8,128)} %copy-done.11) | copy-start | bytes 2359300
  561.5 7.8 collective-permute-start.12
  563.7 5.7 collective-permute-start.15
  565.8 8.7 collective-permute-start.14
  568.1 8.7 collective-permute-start.13
  687.8 36.4 %copy-start.6 = (f32[1536,128]{0,1:T(8,128)S(1)}, f32[1536,128]{0,1:T(8,128)}, u32[]{:S(2)}) copy-start(f32[1536,128]{0,1:T(8,128)} %copy-done.5) | copy-start | bytes 2359300
  693.0 111.8 %copy-start.14 = (f32[1536,128]{0,1:T(8,128)S(1)}, f32[1536,128]{0,1:T(8,128)}, u32[]{:S(2)}) copy-start(f32[1536,128]{0,1:T(8,128)} %fusion.12) | copy-start | bytes 2359300
  694.5 8.3 collective-permute-start.16
  695.9 7.0 collective-permute-start.19
  699.6 7.0 collective-permute-start.18
  701.5 9.2 collective-permute-start.17
  975.2 116.1 %copy-start.7 = (f32[1536,128]{0,1:T(8,128)S(1)}, f32[1536,128]{0,1:T(8,128)}, u32[]{:S(2)}) copy-start(f32[1536,128]{0,1:T(8,128)} %copy-done.5) | copy-start | bytes 2359300
  978.9 112.5 %copy-start.10 = (f32[1536,128]{0,1:T(8,128)S(1)}, f32[1536,128]{0,1:T(8,128)}, u32[]{:S(2)}) copy-start(f32[1536,128]{0,1:T(8,128)} %copy-done.9) | copy-start | bytes 2359300
  980.5 7.8 collective-permute-start.20
  982.6 5.7 collective-permute-start.23
  984.8 8.7 collective-permute-start.22
  987.0 8.7 collective-permute-start.21
  1107.0 115.8 %copy-start.4 = (f32[1536,128]{0,1:T(8,128)S(1)}, f32[1536,128]{0,1:T(8,128)}, u32[]{:S(2)}) copy-start(f32[1536,128]{0,1:T(8,128)} %copy-done.2) | copy-start | bytes 2359300
  1110.7 112.1 %copy-start.8 = (f32[1536,128]{0,1:T(8,128)S(1)}, f32[1536,128]{0,1:T(8,128)}, u32[]{:S(2)}) copy-start(f32[1536,128]{0,1:T(8,128)} %copy-done.5) | copy-start | bytes 2359300
  1112.2 8.5 collective-permute-start.24
  1113.5 7.2 collective-permute-start.27
  1117.2 7.0 collective-permute-start.26
  1119.2 9.2 collective-permute-start.25
  (6 other events, 20.0 us)
Sparse Core Ops, SparseCore 0:
  43.5 147.7 all-reduce.4
  389.4 139.2 all-reduce.6
  808.1 139.2 all-reduce.8
where the time goes:
time: 1250 us; the launch traced here: 1240 us
  waiting for transfers between devices  470 us (38%)
  blocking collectives  465 us (37%)
  other arithmetic  113 us (9%)
  matrix products  60.5 us (5%)
  starting transfers between devices  60.1 us (5%)
  local copies, waits for them, and re-layouts  53.1 us (4%)
  between operations  15.3 us (1%)
    psum x3, waiting for transfers between devices, precondition(): corner_residual = lax.psum(partial_res, 'sub')  426 us
    psum x3, blocking collectives, precondition(): lax.psum(jnp.sum(vector * precond, axis=0), ('cluster', 'sub'))  244 us
    psum x2, blocking collectives, body(): lax.psum(jnp.sum(search * image, axis=0), ('cluster', 'sub'))  158 us
    scatter-add x7, other arithmetic, jump(): jnp.zeros_like(vector).at[flat_ids]  68.4 us
    psum x3, blocking collectives, precondition(): global_res = lax.psum(product(lift_map, corner_residual), 'cluster')  63.1 us
    dot_general x33, matrix products, product(): jnp.dot(left, right, precision=HIGHEST_ACCURACY, preferred_element_type=j...  60.5 us
    ppermute x14, starting transfers between devices, with_halo(): lax.ppermute(lax.slice_in_dim(block, block.shape[dim] - width, None, axis...  30.6 us
    ppermute x14, starting transfers between devices, with_halo(): lax.ppermute(lax.slice_in_dim(block, 0, width, axis=dim), axis, backward)  29 us
  transfers between devices with their start and end apart: 31, of which 15 were waited for; matrix products, arithmetic and copies ran while one was open for 1% of the time, Pallas kernels for 0%

commit v1 on v0

v1 whole, which is shorter than its diff:
```python
import functools

import jax
import jax.numpy as jnp
from jax import lax
from jax.experimental import pallas as pl
from jax.experimental.pallas import tpu as pltpu
from jax.sharding import PartitionSpec as P

F32 = jnp.float32
BF16 = jnp.bfloat16
VMEM_LIMIT = 12 * 1024 * 1024
OPERATOR_VMEM = 24 * 1024 * 1024
PACK_VMEM = 60 * 1024 * 1024
CID_LANE = 25
SCALE_LANE = 24
MAP_LANE = 32
ROWS_AT_ONCE = 8
CHUNK = 128
BLOCK_ROWS = 32


def dot(left, right, contract=((1,), (0,))):
    return lax.dot_general(
        left, right, (contract, ((), ())), precision=lax.Precision.HIGHEST, preferred_element_type=F32
    )


def call(kernel, outs, vmem, smem=(), scratch=(), name=None, flops=0):
    specs = [pl.BlockSpec(memory_space=pltpu.SMEM)] * len(smem)
    specs += [pl.BlockSpec(memory_space=pltpu.VMEM)] * len(vmem)
    moved = sum(a.size * a.dtype.itemsize for a in vmem) + sum(o.size * o.dtype.itemsize for o in outs)
    return pl.pallas_call(
        kernel,
        out_shape=outs,
        in_specs=specs,
        out_specs=[pl.BlockSpec(memory_space=pltpu.VMEM)] * len(outs),
        scratch_shapes=list(scratch),
        compiler_params=pltpu.CompilerParams(vmem_limit_bytes=VMEM_LIMIT),
        cost_estimate=pl.CostEstimate(flops=flops, bytes_accessed=moved, transcendentals=0),
        name=name,
    )(*smem, *vmem)


def out(*shape, dtype=F32):
    return jax.ShapeDtypeStruct(shape, dtype)


def halves(value):
    high = value.astype(BF16)
    return high, (value - high.astype(F32)).astype(BF16)


def dot16(left, right):
    return jnp.dot(left, right, preferred_element_type=F32)


def live_block(count, slot, lanes):
    return lax.broadcasted_iota(jnp.int32, (slot, lanes), 0) < count


def block_of(place, block):
    return place[2 + block]


def pack_kernel(
    place, idx, rhs, basis, scaling, corners, cmap, pa, pb, pc, pd, crow, wide, static, cpad
):
    cdof = basis.shape[0]
    slot = pa.shape[0] // 2
    lanes = pa.shape[1]
    wide[...] = jnp.zeros_like(wide)
    wide[0:cdof, :] = basis[...]
    wide[SCALE_LANE : SCALE_LANE + 1, :] = scaling[...]
    static[...] = wide[...].T
    cpad[...] = jnp.zeros_like(cpad)
    cpad[MAP_LANE : MAP_LANE + cmap.shape[0], :] = cmap[...]
    row = corners[...].astype(F32)
    lane = lax.broadcasted_iota(jnp.int32, (cdof, cdof), 1)
    ids = jnp.sum(
        jnp.where(lane == lax.broadcasted_iota(jnp.int32, (cdof, cdof), 0), row, 0.0),
        axis=1,
        keepdims=True,
    )
    onehot = jnp.where(
        ids == lax.broadcasted_iota(jnp.int32, (cdof, cpad.shape[1]), 1).astype(F32), 1.0, 0.0
    ).astype(F32)
    extra = dot(onehot, cpad[...], ((1,), (1,)))
    lane = lax.broadcasted_iota(jnp.int32, extra.shape, 1)
    extra = jnp.where(lane == CID_LANE, ids, extra)
    lane = lax.broadcasted_iota(jnp.int32, (8, lanes), 1)
    crow[...] = jnp.where((lane >= cdof) & (lane < BLOCK_ROWS), -1.0, 0.0)
    crow[0:1, 0:cdof] = row
    crow[...] = pltpu.roll(crow[...], place[6] * BLOCK_ROWS, 1)
    for block, ref in enumerate((pa, pb, pc, pd)):

        def move(step, carry, block=block, ref=ref):
            base = step * ROWS_AT_ONCE
            for r in range(ROWS_AT_ONCE):
                row = idx[block * slot + base + r]
                ref[pl.ds(base + r, 1), :] = rhs[pl.ds(row, 1), :]
                ref[pl.ds(slot + base + r, 1), :] = static[pl.ds(row, 1), :]
            return carry

        lax.fori_loop(0, slot // ROWS_AT_ONCE, move, 0)
        ref[slot : slot + cdof, :] = ref[slot : slot + cdof, :] + extra


def pack_rows(place, idx, rhs, basis, scaling, corners, cmap, slot):
    order, lanes = rhs.shape
    vmem = (rhs, basis, scaling, corners, cmap)
    outs = [out(2 * slot, lanes)] * 4 + [out(8, lanes)]
    whole = lambda array: pl.BlockSpec(array.shape, lambda i: (0, 0))
    return pl.pallas_call(
        pack_kernel,
        out_shape=outs,
        grid=(1,),
        in_specs=[pl.BlockSpec(memory_space=pltpu.SMEM)] * 2 + [whole(a) for a in vmem],
        out_specs=[pl.BlockSpec(memory_space=pltpu.VMEM)] * len(outs),
        scratch_shapes=[
            pltpu.VMEM((128, order), F32),
            pltpu.VMEM((order, 128), F32),
            pltpu.VMEM((128, cmap.shape[1]), F32),
        ],
        compiler_params=pltpu.CompilerParams(vmem_limit_bytes=PACK_VMEM),
        name="pack",
    )(place, idx, *vmem)


def own_kernel(place, cnt, pa, pb, pc, pd, ct2):
    slot = pa.shape[0] // 2
    for block, mine in enumerate((pa, pb, pc, pd)):
        rows = slice(block * slot, (block + 1) * slot)
        stat = mine[slot : 2 * slot, :]
        lane = lax.broadcasted_iota(jnp.int32, stat.shape, 1)
        live = live_block(cnt[block_of(place, block)], slot, stat.shape[1])
        basis = jnp.where((lane < SCALE_LANE) & live, stat, 0.0).T[0:BLOCK_ROWS, :]
        high, low = halves(basis)
        ct2[0:BLOCK_ROWS, rows] = high
        ct2[BLOCK_ROWS : 2 * BLOCK_ROWS, rows] = low


def restricted(ct2, w2):
    lanes = w2.shape[1] // 2
    both = dot16(ct2[...], w2[...])
    return both[0:BLOCK_ROWS, 0:lanes] + (
        both[0:BLOCK_ROWS, lanes : 2 * lanes] + both[BLOCK_ROWS : 2 * BLOCK_ROWS, 0:lanes]
    )


def send(pay, values, crow, sums):
    cdof = SCALE_LANE
    pay[0] = values
    pay[0, cdof : cdof + 1, :] = crow[0:1, :]
    for at, value in enumerate(sums):
        row = cdof + 1 + at
        pay[0, row : row + 1, :] = column_sum(value)
    message = pay[0]
    for other in range(1, pay.shape[0]):
        pay[other] = message


def sweep(slot):
    for block in range(4):
        for start in range(0, slot, CHUNK):
            yield block, slice(start, start + CHUNK), slice(
                block * slot + start, block * slot + start + CHUNK
            )


def live_chunk(place, cnt, block, rows, lanes):
    row = lax.broadcasted_iota(jnp.int32, (CHUNK, lanes), 0) + rows.start
    return row < cnt[block_of(place, block)]


def first_kernel(place, cnt, crow, pa, pb, pc, pd, qa, qb, qc, qd, ct2, r0, pay, w2):
    slot = pa.shape[0] // 2
    lanes = pa.shape[1]
    mine, theirs = (pa, pb, pc, pd), (qa, qb, qc, qd)
    for block, part, rows in sweep(slot):
        live = live_chunk(place, cnt, block, part, lanes)
        value = jnp.where(live, mine[block][part, :] - theirs[block][part, :], 0.0)
        r0[rows, :] = value
        w2[rows, 0:lanes], w2[rows, lanes : 2 * lanes] = halves(value)
    send(pay, restricted(ct2, w2), crow, [])


def static_kernel(place, cnt, pa, pb, pc, pd, qa, qb, qc, qd, r0, gpad, fts, ft, dsum, dsw, ng, nq):
    slot = pa.shape[0] // 2
    cdof = SCALE_LANE
    lanes = pa.shape[1]
    lane = lax.broadcasted_iota(jnp.int32, (CHUNK, lanes), 1)
    own = lane < cdof
    mine, theirs = (pa, pb, pc, pd), (qa, qb, qc, qd)
    nq[...] = jnp.zeros_like(nq)
    nq[0:cdof, :] = pa[slot : slot + cdof, :]
    for block in range(4):
        start = cdof * (block + 1)
        nq[start : start + cdof, :] = theirs[block][slot : slot + cdof, :]
    ng[...] = dot(nq[...], gpad[...])
    for block, part, rows in sweep(slot):
        live = live_chunk(place, cnt, block, part, lanes)
        low_rows = slice(slot + part.start, slot + part.stop)
        stat = mine[block][low_rows, :]
        other = theirs[block][low_rows, :]
        basis_mine = jnp.where(own & live, stat, 0.0)
        basis_other = jnp.where(own & live, other, 0.0)
        full = basis_mine - pltpu.roll(basis_other, cdof * (block + 1), 1)
        fts[rows, 0:lanes], fts[rows, lanes : 2 * lanes] = halves(full)
        ft[rows, :] = full
        weight = jnp.sum(
            jnp.where((lane == cdof) & live, stat + other, 0.0), axis=1, keepdims=True
        )
        weight = jnp.broadcast_to(weight, (CHUNK, lanes))
        dsum[rows, :] = weight
        dsw[rows, :] = weight * r0[rows, :]


def coarse_kernel(factor, ginv, coarse, gpad):
    gdof = ginv.shape[0]
    coarse[...] = dot(factor[...], factor[...], ((0,), (0,)))
    gpad[...] = jnp.zeros_like(gpad)
    gpad[MAP_LANE : MAP_LANE + gdof, :] = dot(ginv[...], ginv[...], ((0,), (0,)))


def split_kernel(x, split):
    lanes = x.shape[1]
    for start in range(0, x.shape[0], CHUNK):
        rows = slice(start, start + CHUNK)
        split[rows, 0:lanes], split[rows, lanes : 2 * lanes] = halves(x[rows, :])


def go_home(idx, pairs):
    def move(at, carry):
        base = at * ROWS_AT_ONCE
        for r in range(ROWS_AT_ONCE):
            row = idx[base + r]
            for source, target in pairs:
                target[pl.ds(row, 1), :] = source[pl.ds(base + r, 1), :]
        return carry

    lax.fori_loop(0, idx.shape[0] // ROWS_AT_ONCE, move, 0)


def halves_kernel(b, b2):
    rows = b.shape[1]
    b2[:, 0:rows], b2[:, rows : 2 * rows] = halves(b[...])


def split_operator(operator):
    rows = operator.shape[0]
    tile = 256
    return pl.pallas_call(
        halves_kernel,
        out_shape=out(rows, 2 * rows, dtype=BF16),
        grid=(rows // tile,),
        in_specs=[pl.BlockSpec((tile, rows), lambda i: (i, 0))],
        out_specs=pl.BlockSpec((tile, 2 * rows), lambda i: (i, 0)),
        compiler_params=pltpu.CompilerParams(vmem_limit_bytes=OPERATOR_VMEM),
        cost_estimate=pl.CostEstimate(
            flops=0, bytes_accessed=8 * rows * rows, transcendentals=0
        ),
        name="halves",
    )(operator)


def operator_kernel(idx, x, b2, o, natural, split):
    rows, n = x.shape
    tile = rows // 2
    go_home(idx, ((x, natural),))
    for start in range(0, rows, CHUNK):
        part = slice(start, start + CHUNK)
        low_part = slice(rows + start, rows + start + CHUNK)
        high, low = halves(natural[part, :])
        split[part, 0:n] = high
        split[part, n : 2 * n] = low
        split[low_part, 0:n] = high
        split[low_part, n : 2 * n] = jnp.zeros((CHUNK, n), BF16)

    def multiply(at, carry):
        part = pl.ds(at * tile, tile)
        both = dot16(b2[part, :], split[...])
        natural[part, :] = both[:, 0:n] + both[:, n : 2 * n]
        return carry

    lax.fori_loop(0, rows // tile, multiply, 0)

    def move(at, carry):
        base = at * ROWS_AT_ONCE
        for r in range(ROWS_AT_ONCE):
            o[pl.ds(base + r, 1), :] = natural[pl.ds(idx[base + r], 1), :]
        return carry

    lax.fori_loop(0, rows // ROWS_AT_ONCE, move, 0)


def apply_operator(idx, x, b2):
    rows, n = x.shape
    (result,) = call(
        operator_kernel,
        [out(rows, n)],
        [x, b2],
        smem=[idx],
        scratch=[pltpu.VMEM((rows, n), F32), pltpu.VMEM((2 * rows, 2 * n), BF16)],
        name="operator",
        flops=6 * rows * rows * n,
    )
    return result


def gathered_product(y, table, p1, cvab):
    subs, rows, lanes = y.shape
    value = y[...].reshape(subs * rows, lanes)
    high, low = halves(value)
    both = dot16(table[...], jnp.concatenate([high, low], axis=1))
    half = both.shape[0] // 2
    total = both[0:half, 0:lanes] + (both[0:half, lanes:] + both[half:, 0:lanes])
    top = p1.shape[0]
    p1[...] = total[0:top, :]
    cvab[...] = total[top:, :]


def table_kernel(y, pa, qa, qb, coarse, cmap, table, p1, cvab, reach2):
    subs, rows, lanes = y.shape
    cdof = SCALE_LANE
    slot = pa.shape[0] // 2
    gdof, ccl = cmap.shape
    number = lax.broadcasted_iota(jnp.int32, (cdof, ccl), 1).astype(F32)
    chosen = [
        jnp.where(ref[slot : slot + cdof, CID_LANE : CID_LANE + 1] == number, 1.0, 0.0)
        for ref in (pa, qa, qb)
    ]
    reach = jnp.concatenate(
        [cmap[...], jnp.zeros((8, ccl), F32), dot(jnp.concatenate(chosen, axis=0), coarse[...])],
        axis=0,
    )
    reach2[0:128, :], reach2[128:256, :] = halves(reach)
    per = lanes // rows
    which = lax.broadcasted_iota(jnp.int32, (ccl, lanes), 0).astype(F32)
    row = lax.broadcasted_iota(jnp.int32, (256, lanes), 0)
    column = lax.broadcasted_iota(jnp.int32, (256, lanes), 1) % rows
    kept = (row - gdof == column - cdof) & (row > gdof) & (row < gdof + 8)
    unit = jnp.where(kept, 1.0, 0.0)
    for group in range(subs // per):
        ids = y[group * per, cdof : cdof + 1, :]
        for r in range(1, per):
            ids = ids + y[group * per + r, cdof : cdof + 1, :]
        onehot = jnp.where(which == ids, 1.0, 0.0).astype(BF16)
        at = slice(group * lanes, (group + 1) * lanes)
        table[:, at] = (dot16(reach2[...], onehot) + unit).astype(BF16)
    gathered_product(y, table, p1, cvab)


def corner_kernel(y, table, p1, cvab):
    gathered_product(y, table, p1, cvab)


def pair_kernel(place, own, other, p2):
    cdof = SCALE_LANE
    top = own.shape[0] - cdof
    odd = place[0] == 1
    p2[0:top, :] = own[0:top, :] + other[0:top, :]
    mine = own[top : top + cdof, :]
    theirs = other[top : top + cdof, :]
    p2[top : top + cdof, :] = jnp.where(odd, theirs, mine)
    p2[top + cdof : top + 2 * cdof, :] = jnp.where(odd, mine, theirs)


def corner_values(place, p2, c2, c4, c6, cvab, ng, cv, cv2):
    cdof = SCALE_LANE
    top = p2.shape[0] - 2 * cdof
    gdof = top - 8
    lanes = cv.shape[1]
    even = slice(top, top + cdof)
    odd = slice(top + cdof, top + 2 * cdof)
    is_odd = place[0] == 1
    total = (p2[0:top, :] + c2[0:top, :]) + (c4[0:top, :] + c6[0:top, :])
    cv[0:cdof, :] = jnp.where(is_odd, p2[odd, :], p2[even, :])
    cv[cdof : 3 * cdof, :] = cvab[...]
    cv[3 * cdof : 4 * cdof, :] = jnp.where(is_odd, p2[even, :], p2[odd, :])
    far = place[1] == 1
    cv[4 * cdof : 5 * cdof, :] = jnp.where(
        is_odd,
        jnp.where(far, c6[even, :], c2[even, :]),
        jnp.where(far, c6[odd, :], c2[odd, :]),
    )
    cv[5 * cdof : 128, :] = jnp.zeros((128 - 5 * cdof, lanes), F32)
    high, low = halves(cv[...] + dot(ng[...], total[0:gdof, :]))
    cv2[0:128, 0:lanes] = high
    cv2[128:256, 0:lanes] = high
    cv2[0:128, lanes : 2 * lanes] = low
    cv2[128:256, lanes : 2 * lanes] = jnp.zeros((128, lanes), BF16)
    return total[gdof : gdof + 8, :]


def times_corner(matrix, rows, cv2):
    both = dot16(matrix[rows, :], cv2[...])
    lanes = both.shape[1] // 2
    return both[:, 0:lanes] + both[:, lanes:]


def column_sum(value):
    return jnp.sum(value, axis=0, keepdims=True)


def stage0_kernel(
    place, p2, c2, c4, c6, cvab, ng, t, dsw, fts, bfs, v0, ua, ub, uc, ud, cv, cv2
):
    corner_values(place, p2, c2, c4, c6, cvab, ng, cv, cv2)
    lanes = cv.shape[1]
    blocks = (ua, ub, uc, ud)
    for block, part, rows in sweep(ua.shape[0]):
        v0[rows, :] = dsw[rows, :] + times_corner(fts, rows, cv2)
        blocks[block][part, :] = t[rows, :] + times_corner(bfs, rows, cv2)


def stage1_kernel(
    place, p2, c2, c4, c6, cvab, ng, fts, bfs, t, dsw, v0, r0, w0,
    u0a, u0b, u0c, u0d, v1, bv1, z1, r1, scal, ua, ub, uc, ud, cv, cv2,
):
    dots = corner_values(place, p2, c2, c4, c6, cvab, ng, cv, cv2)
    alpha = dots[1:2, :] / dots[2:3, :]
    scal[...] = dots
    scal[0:1, :] = alpha
    olds, news = (u0a, u0b, u0c, u0d), (ua, ub, uc, ud)
    for block, part, rows in sweep(ua.shape[0]):
        new = dsw[rows, :] + times_corner(fts, rows, cv2)
        v1[rows, :] = new
        z1[rows, :] = v0[rows, :] - alpha * new
        r1[rows, :] = r0[rows, :] - alpha * w0[rows, :]
        image = t[rows, :] + times_corner(bfs, rows, cv2)
        bv1[rows, :] = image
        news[block][part, :] = olds[block][part, :] - alpha * image


def stage2_kernel(
    place, p2, c2, c4, c6, cvab, ng, fts, bfs, t, dsw, v0, w0, v1, bv1, z1, r1, s1, scal,
    u1a, u1b, u1c, u1d, z2, p1, r2, q1, scal2, dots2, ua, ub, uc, ud, cv, cv2,
):
    dots = corner_values(place, p2, c2, c4, c6, cvab, ng, cv, cv2)
    lanes = cv.shape[1]
    rz0 = scal[1:2, :]
    pq0 = scal[2:3, :]
    rz1 = dots[1:2, :]
    beta = rz1 / rz0
    pq1 = dots[2:3, :] + beta * (dots[3:4, :] + dots[4:5, :]) + beta * beta * pq0
    alpha = rz1 / pq1
    scal2[...] = jnp.zeros_like(scal2)
    scal2[0:1, :] = scal[0:1, :]
    scal2[1:2, :] = rz1
    scal2[2:3, :] = pq1
    scal2[3:4, :] = alpha
    olds, news = (u1a, u1b, u1c, u1d), (ua, ub, uc, ud)
    sums = [jnp.zeros((8, lanes), F32) for _ in range(4)]

    def folded(value):
        return jnp.sum(value.reshape(CHUNK // 8, 8, lanes), axis=0)

    for block, part, rows in sweep(ua.shape[0]):
        search = z1[rows, :] + beta * v0[rows, :]
        p1[rows, :] = search
        image_q = s1[rows, :] + beta * w0[rows, :]
        q1[rows, :] = image_q
        res = r1[rows, :] - alpha * image_q
        r2[rows, :] = res
        new = z1[rows, :] - alpha * (
            dsw[rows, :] + times_corner(fts, rows, cv2) + beta * v1[rows, :]
        )
        z2[rows, :] = new
        image = t[rows, :] + times_corner(bfs, rows, cv2) + beta * bv1[rows, :]
        fresh = olds[block][part, :] - alpha * image
        news[block][part, :] = fresh
        sums[0] = sums[0] + folded(res * new)
        sums[1] = sums[1] + folded(fresh * new)
        sums[2] = sums[2] + folded(image_q * new)
        sums[3] = sums[3] + folded(fresh * search)
    dots2[0] = jnp.zeros((8, lanes), F32)
    dots2[0, 1:2, :] = column_sum(sums[0])
    dots2[0, 2:3, :] = 2.0 * column_sum(sums[1])
    dots2[0, 3:4, :] = column_sum(sums[2])
    dots2[0, 4:5, :] = 2.0 * column_sum(sums[3])
    message = dots2[0]
    for other in range(1, dots2.shape[0]):
        dots2[other] = message


def jump_kernel(pairs, place, cnt, ua, ub, uc, ud, qa, qb, qc, qd, dsum, ct2, crow, *rest):
    fields, (w, dsw, pay, w2) = rest[:-4], rest[-4:]
    lanes = w.shape[1]
    mine, theirs = (ua, ub, uc, ud), (qa, qb, qc, qd)
    sums = [jnp.zeros((8, lanes), F32) for _ in pairs]
    for block, part, rows in sweep(ua.shape[0]):
        live = live_chunk(place, cnt, block, part, lanes)
        value = jnp.where(live, mine[block][part, :] - theirs[block][part, :], 0.0)
        w[rows, :] = value
        dsw[rows, :] = dsum[rows, :] * value
        w2[rows, 0:lanes], w2[rows, lanes : 2 * lanes] = halves(value)
        for at, (left, right) in enumerate(pairs):
            first = value if left < 0 else fields[left][rows, :]
            product = first * fields[right][rows, :]
            sums[at] = sums[at] + jnp.sum(product.reshape(CHUNK // 8, 8, lanes), axis=0)
    send(pay, restricted(ct2, w2), crow, sums)


def sum_kernel(x, o):
    o[...] = jnp.sum(x[...], axis=0)


def add_kernel(x, y, o):
    o[...] = x[...] + y[...]


def home_kernel(idx, scal2, z2, p1, r2, q1, v0, z2n, p1n, r2n, q1n, xsn, xs):
    xs[...] = scal2[0:1, :] * v0[...] + scal2[3:4, :] * p1[...]

    go_home(idx, ((z2, z2n), (p1, p1n), (r2, r2n), (q1, q1n), (xs, xsn)))


def home_jump_kernel(place, cnt, idx, ua, ub, uc, ud, qa, qb, qc, qd, s2n, s2):
    lanes = s2.shape[1]
    mine, theirs = (ua, ub, uc, ud), (qa, qb, qc, qd)
    for block, part, rows in sweep(ua.shape[0]):
        live = live_chunk(place, cnt, block, part, lanes)
        s2[rows, :] = jnp.where(live, mine[block][part, :] - theirs[block][part, :], 0.0)

    go_home(idx, ((s2, s2n),))


def last_kernel(z2, p1, r2, q1, xs, s2, scal2, d0, d2, d4, d6, mult, resid):
    dots = (d0[...] + d2[...]) + (d4[...] + d6[...])
    beta = dots[1:2, :] / scal2[1:2, :]
    pq = dots[2:3, :] + beta * (dots[3:4, :] + dots[4:5, :]) + beta * beta * scal2[2:3, :]
    alpha = dots[1:2, :] / pq
    for start in range(0, z2.shape[0], CHUNK):
        rows = slice(start, start + CHUNK)
        mult[rows, :] = xs[rows, :] + alpha * (z2[rows, :] + beta * p1[rows, :])
        resid[rows, :] = r2[rows, :] - alpha * (s2[rows, :] + beta * q1[rows, :])


def body(
    dual_ops,
    rhs,
    corner_basis,
    scaling,
    cluster_corner_inverse,
    coarse_map,
    global_inv,
    row_index,
    pair_counts,
    corner_map,
):
    operator = dual_ops[0, 0]
    loads = rhs[0, 0]
    basis = corner_basis[0, 0]
    weights = scaling[0]
    factor = cluster_corner_inverse[0]
    lift_map = coarse_map[0]
    row_ids = row_index[0, 0]
    cnt = pair_counts[0, 0]
    corners = corner_map[0]
    slot = row_ids.shape[1]
    order, lanes = loads.shape
    cdof = basis.shape[0]
    subs = lax.axis_size("sub")
    clusters = lax.axis_size("cluster")
    gdof = lift_map.shape[0]

    s = lax.axis_index("sub")
    c = lax.axis_index("cluster")
    s_odd = s % 2
    c_odd = c % 2
    pairs_a = [(i, i ^ 1) for i in range(subs)]
    pairs_b = [(i, i + 1) for i in range(1, subs - 1, 2)]
    pairs_b += [(j, i) for i, j in pairs_b]
    pairs_c = [(i, i ^ 1) for i in range(clusters)]
    pairs_d = [(i, i + 1) for i in range(1, clusters - 1, 2)]
    pairs_d += [(j, i) for i, j in pairs_d]
    across = [[(i, i ^ k) for i in range(clusters)] for k in (2, 4, 6)]

    chip = c // 2
    next_chip = jnp.where(c_odd == 1, chip + 1, chip - 1)
    far = ((chip ^ next_chip) == 3).astype(jnp.int32)
    sides = [1 - s_odd, s_odd, 3 - c_odd, 2 + c_odd]
    place = jnp.stack(
        [v.astype(jnp.int32) for v in (c_odd, far, *sides, s % (lanes // BLOCK_ROWS), far)]
    )

    idx = jnp.concatenate(
        [
            jnp.where(s_odd == 0, row_ids[1], row_ids[0]),
            jnp.where(s_odd == 0, row_ids[0], row_ids[1]),
            jnp.where(c_odd == 0, row_ids[3], row_ids[2]),
            jnp.where(c_odd == 0, row_ids[2], row_ids[3]),
        ]
    )

    def exchange(blocks):
        return [
            lax.ppermute(blocks[0], "sub", pairs_a),
            lax.ppermute(blocks[1], "sub", pairs_b),
            lax.ppermute(blocks[2], "cluster", pairs_c),
            lax.ppermute(blocks[3], "cluster", pairs_d),
        ]

    def spread(messages):
        return lax.all_to_all(messages, "sub", 0, 0, tiled=True)

    def together(*values):
        return lax.optimization_barrier(values)

    def clusterwise(p1, cvab):
        other = lax.ppermute(p1, "cluster", pairs_c)
        (p2,) = call(
            pair_kernel,
            [out(gdof + 8 + 2 * cdof, lanes)],
            [p1, other],
            smem=[place],
            name="pair",
        )
        moved = [lax.ppermute(p2, "cluster", k) for k in across]
        return [p2, *moved, cvab]

    block_out = [out(slot, lanes)] * 4
    full = out(order, lanes)
    small = [out(gdof + 8 + cdof, lanes), out(2 * cdof, lanes)]
    cv_scratch = [pltpu.VMEM((128, lanes), F32), pltpu.VMEM((256, 2 * lanes), BF16)]
    w2_scratch = [pltpu.VMEM((order, 2 * lanes), BF16)]

    *packs, crow = pack_rows(place, idx, loads, basis, weights, corners, lift_map, slot)
    packs_in = exchange(packs)
    (ct2,) = call(
        own_kernel, [out(2 * BLOCK_ROWS, order, dtype=BF16)], [*packs], smem=[place, cnt], name="own"
    )
    coarse, gpad = call(
        coarse_kernel,
        [out(*factor.shape), out(128, gdof)],
        [factor, global_inv],
        name="coarse",
    )
    b2 = split_operator(operator)
    b2, ct2, coarse, gpad, *packs_in = together(b2, ct2, coarse, gpad, *packs_in)
    r0, pay = call(
        first_kernel,
        [full, out(subs, BLOCK_ROWS, lanes)],
        [crow, *packs, *packs_in, ct2],
        smem=[place, cnt],
        scratch=w2_scratch,
        name="first",
    )

    y = spread(pay)
    y, r0 = together(y, r0)
    table, p1, cvab = call(
        table_kernel,
        [out(256, subs * BLOCK_ROWS, dtype=BF16)] + small,
        [y, packs[0], *packs_in[:2], coarse, lift_map],
        scratch=[pltpu.VMEM((256, factor.shape[0]), BF16)],
        name="table",
    )
    cluster_part = clusterwise(p1, cvab)
    fts, ft, dsum, dsw, ng = call(
        static_kernel,
        [
            out(order, 2 * lanes, dtype=BF16),
            full,
            full,
            full,
            out(128, gdof),
        ],
        [*packs, *packs_in, r0, gpad],
        smem=[place, cnt],
        scratch=[pltpu.VMEM((128, lanes), F32)],
        name="static",
    )
    t = apply_operator(idx, dsw, b2)
    bf = apply_operator(idx, ft, b2)
    (bfs,) = call(split_kernel, [out(order, 2 * lanes, dtype=BF16)], [bf], name="split")
    v0, *u0 = call(
        stage0_kernel,
        [full] + block_out,
        [*cluster_part, ng, t, dsw, fts, bfs],
        smem=[place],
        scratch=cv_scratch,
        name="stage0",
    )
    w0, dsw, pay = call(
        functools.partial(jump_kernel, ((0, 1), (-1, 1))),
        [full, full, out(subs, BLOCK_ROWS, lanes)],
        [*u0, *exchange(u0), dsum, ct2, crow, r0, v0],
        smem=[place, cnt],
        scratch=w2_scratch,
        name="jump1",
    )

    y = spread(pay)
    y, dsw = together(y, dsw)
    p1, cvab = call(corner_kernel, small, [y, table], name="corner")
    cluster_part = clusterwise(p1, cvab)
    t = apply_operator(idx, dsw, b2)
    v1, bv1, z1, r1, scal, *u1 = call(
        stage1_kernel,
        [full] * 4 + [out(8, lanes)] + block_out,
        [*cluster_part, ng, fts, bfs, t, dsw, v0, r0, w0, *u0],
        smem=[place],
        scratch=cv_scratch,
        name="stage1",
    )
    s1, dsw, pay = call(
        functools.partial(jump_kernel, ((0, 1), (-1, 1), (2, 1), (-1, 3))),
        [full, full, out(subs, BLOCK_ROWS, lanes)],
        [*u1, *exchange(u1), dsum, ct2, crow, r1, z1, w0, v0],
        smem=[place, cnt],
        scratch=w2_scratch,
        name="jump2",
    )

    y = spread(pay)
    y, dsw = together(y, dsw)
    p1, cvab = call(corner_kernel, small, [y, table], name="corner")
    cluster_part = clusterwise(p1, cvab)
    t = apply_operator(idx, dsw, b2)
    z2, p1, r2, q1, scal2, dots2, *u2 = call(
        stage2_kernel,
        [full] * 4 + [out(8, lanes), out(subs, 8, lanes)] + block_out,
        [*cluster_part, ng, fts, bfs, t, dsw, v0, w0, v1, bv1, z1, r1, s1, scal, *u1],
        smem=[place],
        scratch=cv_scratch,
        name="stage2",
    )

    dots = spread(dots2)
    dots, z2, scal2, *u2 = together(dots, z2, scal2, *u2)
    u2_in = exchange(u2)
    (dots,) = call(sum_kernel, [out(8, lanes)], [dots], name="sum")
    other = lax.ppermute(dots, "cluster", pairs_c)
    (dots,) = call(add_kernel, [out(8, lanes)], [dots, other], name="add")
    moved = [lax.ppermute(dots, "cluster", k) for k in across]
    home = call(
        home_kernel,
        [full] * 5,
        [scal2, z2, p1, r2, q1, v0],
        smem=[idx],
        scratch=[pltpu.VMEM((order, lanes), F32)],
        name="home",
    )
    (s2,) = call(
        home_jump_kernel,
        [full],
        [*u2, *u2_in],
        smem=[place, cnt, idx],
        scratch=[pltpu.VMEM((order, lanes), F32)],
        name="home_jump",
    )
    multipliers, residual = call(
        last_kernel,
        [full, full],
        [*home, s2, scal2, dots, *moved],
        name="last",
    )
    return (multipliers[None, None], residual[None, None])


def solution(mesh):
    in_specs = (
        P("cluster", "sub", None, None),
        P("cluster", "sub", None, None),
        P("cluster", "sub", None, None),
        P("cluster", "sub", None),
        P("cluster", None, None),
        P("cluster", None, None),
        P(),
        P("cluster", "sub", None, None),
        P("cluster", "sub", None),
        P("cluster", "sub", None),
    )
    out_specs = (P("cluster", "sub", None, None), P("cluster", "sub", None, None))
    return jax.shard_map(body, mesh=mesh, in_specs=in_specs, out_specs=out_specs, check_vma=False)
```

time: 1250 us -> 223 us (0.18)
  waiting for transfers between devices: 470 us -> 13.2 us
  blocking collectives: 465 us -> 94.7 us
  other arithmetic: 113 us -> 1.48 us
  Pallas kernels: 0 us -> 61.6 us
  matrix products: 60.5 us -> 0 us
  local copies, waits for them, and re-layouts: 53.1 us -> 9.65 us
  starting transfers between devices: 60.1 us -> 37.1 us
  between operations: 15.3 us -> 1.29 us
    psum x8 -> x0, blocking collectives: 465 us -> none  [the longest x3 244 us: precondition(): lax.psum(jnp.sum(vector * precond, axis=0), ('cluster', 'sub'))]
    psum x3 -> x0, waiting for transfers between devices: 426 us -> none  [precondition(): corner_residual = lax.psum(partial_res, 'sub')]
    all_to_all x0 -> x4, blocking collectives: none -> 94.7 us  [spread(): return lax.all_to_all(messages, 'sub', 0, 0, tiled=True)]
    scatter-add x8 -> x0, other arithmetic: 77.1 us -> none  [the longest x7 68.4 us: jump(): jnp.zeros_like(vector).at[flat_ids]]
    pallas_call x0 -> x27, Pallas kernels: none -> 61.6 us  [the longest x25 54.8 us: call(): pl.pallas_call(kernel, out_shape=outs, in_specs=specs, out_specs=[pl.Bloc...]
    dot_general x33 -> x0, matrix products: 60.5 us -> none  [product(): jnp.dot(left, right, precision=HIGHEST_ACCURACY, preferred_element_type=j...]
    ppermute x28 -> x32, waiting for transfers between devices: 43.8 us -> 13.2 us  [the longest x4 5.02 us: exchange(): lax.ppermute(blocks[3], 'cluster', pairs_d)]
    gather x7 -> x0, local copies, waits for them, and re-layouts: 25.9 us -> none  [jump(): slot_vals = vector[row_ids] * live_slot[:, :, None]]
  transfers between devices with their start and end apart: 31 -> 32, of which waited for: 15 -> 7; matrix products, arithmetic and copies ran while one was open for 1% -> 0% of each run, Pallas kernels for 0% -> 19%
where the time goes in v1:
time: 223 us; the launch traced here: 219 us
  blocking collectives  94.7 us (42%)
  Pallas kernels  61.6 us (28%)
  starting transfers between devices  37.1 us (17%)
  waiting for transfers between devices  13.2 us (6%)
  local copies, waits for them, and re-layouts  9.65 us (4%)
    all_to_all x4, blocking collectives, spread(): return lax.all_to_all(messages, 'sub', 0, 0, tiled=True)  94.7 us
    pallas_call x25, Pallas kernels, call(): pl.pallas_call(kernel, out_shape=outs, in_specs=specs, out_specs=[pl.Bloc...  54.8 us
    ppermute x9, starting transfers between devices, clusterwise(): moved = [lax.ppermute(p2, 'cluster', k) for k in across]  12.7 us
    ppermute x4, starting transfers between devices, exchange(): lax.ppermute(blocks[3], 'cluster', pairs_d)  10.2 us
    unnamed x36, local copies, waits for them, and re-layouts  9.02 us
    pallas_call x1, Pallas kernels, pack_rows(): pl.pallas_call(pack_kernel, out_shape=outs, grid=(1,), in_specs=[pl.Block...  5.42 us
    ppermute x4, starting transfers between devices, exchange(): lax.ppermute(blocks[0], 'sub', pairs_a)  5.4 us
    ppermute x4, waiting for transfers between devices, exchange(): lax.ppermute(blocks[3], 'cluster', pairs_d)  5.02 us
  transfers between devices with their start and end apart: 32, of which 7 were waited for; matrix products, arithmetic and copies ran while one was open for 0% of the time, Pallas kernels for 19%

profile of v1, /device:TPU:8, one launch (start us, length us, event | category | flops | bytes accessed | tf_op | source)
XLA Modules:
  0.0 219.0 jit_solution(4717521334760867642)
XLA Ops:
  2.8 5.4 %pack.1 = (f32[768,128]{1,0:T(8,128)}, f32[768,128]{1,0:T(8,128)}, f32[768,128]{1,0:T(8,128)}, f32[768,128]{1,0:T(8,128)}, f32[8,128]{1,0:T(8,128)}) custom-call(s32[8]{0:T(128)} %stack.36.place, s32[1536]{0:T(1024)} %pad_add_fusion.idx, f32[1536,128]{1,0:T(8,128)} %bitcast.27, f32[24,1536]{1,0:T(8,128)} %bitcast.28, f32[1,1536]{1,0:T(1,128)} %bitcast.29, ...), custom_call_target="tpu_custom_call" | custom-call | tf_op jit(solution)/shard_map/pack/pallas_call | solution.py:114
  9.0 4.2 %collective-permute-start.3 = (f32[768,128]{1,0:T(8,128)}, f32[768,128]{1,0:T(8,128)S(1)}, u32[]{:S(2)}, u32[]{:S(2)}) collective-permute-start(f32[768,128]{1,0:T(8,128)} %get-tuple-element.85.pd), channel_id=1, source_target_pairs={{32,64},{96,128},{160,192},{64,32},{128,96},{192,160},{33,65},{97,... | collective-permute-start | bytes 1179656 | tf_op jit(solution)/shard_map/ppermute | solution.py:602
  13.2 2.6 %collective-permute-start = (f32[768,128]{1,0:T(8,128)}, f32[768,128]{1,0:T(8,128)S(1)}, u32[]{:S(2)}, u32[]{:S(2)}) collective-permute-start(f32[768,128]{1,0:T(8,128)} %get-tuple-element.82.pa), channel_id=1, source_target_pairs={{0,1},{1,0},{2,3},{3,2},{4,5},{5,4},{6,7},{7,6},{8,9},{9,8},{10,11... | collective-permute-start | bytes 1179656 | tf_op jit(solution)/shard_map/ppermute | solution.py:599
  15.7 1.0 copy-done.1
  16.8 1.0 copy-done.3
  17.8 1.0 copy-done.5
  21.8 3.7 %copy-done = f32[1,1,1536,1536]{3,2,1,0:T(8,128)S(1)} copy-done((f32[1,1,1536,1536]{3,2,1,0:T(8,128)S(1)}, f32[1,1,1536,1536]{3,2,1,0:T(8,128)}, u32[]{:S(2)}) %copy-start) | copy-done | bytes 9437208
  25.6 1.4 halves.1.b2
  27.0 1.3 coarse.1
  28.5 1.1 first.1
  29.5 28.3 %all_to_all.20.y = f32[32,32,128]{2,1,0:T(8,128)S(1)} all-to-all(f32[32,32,128]{2,1,0:T(8,128)S(1)} %get-tuple-element.93), channel_id=1, replica_groups=mesh['cluster'=8,'sub'=32] {'sub'}, dimensions={0} | all-to-all | bytes 1048576 | tf_op jit(solution)/shard_map/all_to_all | solution.py:606
  57.8 1.2 table.1
  59.2 1.3 static.1
  60.5 7.5 %operator.5.x = f32[1536,128]{1,0:T(8,128)S(1)} custom-call(s32[1536]{0:T(1024)S(1)} %copy-done.10, f32[1536,128]{1,0:T(8,128)S(1)} %get-tuple-element.105.x, bf16[1536,3072]{1,0:T(8,128)(2,1)S(1)} %halves.1.b2), custom_call_target="tpu_custom_call" | custom-call | flops 1811939328 | bytes 11010048 | tf_op jit(solution)/shard_map/operator/pallas_call | solution.py:33
  68.6 2.2 collective-permute-start.7
  70.8 2.2 collective-permute-start.5
  73.0 7.5 %operator.4.t = f32[1536,128]{1,0:T(8,128)S(1)} custom-call(s32[1536]{0:T(1024)S(1)} %copy-done.10, f32[1536,128]{1,0:T(8,128)S(1)} %get-tuple-element.102.x.dsw, bf16[1536,3072]{1,0:T(8,128)(2,1)S(1)} %halves.1.b2), custom_call_target="tpu_custom_call" | custom-call | flops 1811939328 | bytes 11010048 | tf_op jit(solution)/shard_map/operator/pallas_call | solution.py:33
  80.7 1.4 stage0.1
  82.1 1.7 collective-permute-start.8
  84.6 2.0 collective-permute-start.11
  86.6 2.5 %collective-permute-done.8.qa = f32[384,128]{1,0:T(8,128)S(1)} collective-permute-done((f32[384,128]{1,0:T(8,128)S(1)}, f32[384,128]{1,0:T(8,128)S(1)}, u32[]{:S(2)}, u32[]{:S(2)}) %collective-permute-start.8) | collective-permute-done | bytes 196640 | tf_op jit(solution)/shard_map/ppermute | solution.py:599
  89.1 2.5 %collective-permute-done.11.qd = f32[384,128]{1,0:T(8,128)S(1)} collective-permute-done((f32[384,128]{1,0:T(8,128)S(1)}, f32[384,128]{1,0:T(8,128)S(1)}, u32[]{:S(2)}, u32[]{:S(2)}) %collective-permute-start.11) | collective-permute-done | bytes 196640 | tf_op jit(solution)/shard_map/ppermute | solution.py:602
  91.6 1.1 jump1.1
  92.8 25.7 %all_to_all.21.y = f32[32,32,128]{2,1,0:T(8,128)S(1)} all-to-all(f32[32,32,128]{2,1,0:T(8,128)S(1)} %get-tuple-element.112), channel_id=1, replica_groups=mesh['cluster'=8,'sub'=32] {'sub'}, dimensions={0} | all-to-all | bytes 1048576 | tf_op jit(solution)/shard_map/all_to_all | solution.py:606
  118.8 1.2 collective-permute-done.12.other
  120.6 1.4 collective-permute-start.15
  122.9 1.9 collective-permute-start.13
  124.8 7.5 %operator.6.t = f32[1536,128]{1,0:T(8,128)S(1)} custom-call(s32[1536]{0:T(1024)S(1)} %copy-done.10, f32[1536,128]{1,0:T(8,128)S(1)} %get-tuple-element.118.x.dsw, bf16[1536,3072]{1,0:T(8,128)(2,1)S(1)} %halves.1.b2), custom_call_target="tpu_custom_call" | custom-call | flops 1811939328 | bytes 11010048 | tf_op jit(solution)/shard_map/operator/pallas_call | solution.py:33
  132.4 1.6 stage1.1
  135.7 2.0 collective-permute-start.19
  137.7 2.5 %collective-permute-done.16.qa = f32[384,128]{1,0:T(8,128)S(1)} collective-permute-done((f32[384,128]{1,0:T(8,128)S(1)}, f32[384,128]{1,0:T(8,128)S(1)}, u32[]{:S(2)}, u32[]{:S(2)}) %collective-permute-start.16) | collective-permute-done | bytes 196640 | tf_op jit(solution)/shard_map/ppermute | solution.py:599
  140.2 2.5 %collective-permute-done.19.qd = f32[384,128]{1,0:T(8,128)S(1)} collective-permute-done((f32[384,128]{1,0:T(8,128)S(1)}, f32[384,128]{1,0:T(8,128)S(1)}, u32[]{:S(2)}, u32[]{:S(2)}) %collective-permute-start.19) | collective-permute-done | bytes 196640 | tf_op jit(solution)/shard_map/ppermute | solution.py:602
  142.7 1.3 jump2.1
  144.0 25.7 %all_to_all.22.y = f32[32,32,128]{2,1,0:T(8,128)S(1)} all-to-all(f32[32,32,128]{2,1,0:T(8,128)S(1)} %get-tuple-element.126), channel_id=1, replica_groups=mesh['cluster'=8,'sub'=32] {'sub'}, dimensions={0} | all-to-all | bytes 1048576 | tf_op jit(solution)/shard_map/all_to_all | solution.py:606
  170.1 1.2 collective-permute-done.20.other
  171.9 1.4 collective-permute-start.23
  173.3 2.8 %collective-permute-start.21 = (f32[104,128]{1,0:T(8,128)S(1)}, f32[104,128]{1,0:T(8,128)S(1)}, u32[]{:S(2)}, u32[]{:S(2)}) collective-permute-start(f32[104,128]{1,0:T(8,128)S(1)} %pair.5.p2), channel_id=1, source_target_pairs={{0,64},{32,96},{64,0},{96,32},{128,192},{160,224},{192,128},{224,1... | collective-permute-start | bytes 159752 | tf_op jit(solution)/shard_map/ppermute | solution.py:620
  176.1 7.5 %operator.7.t = f32[1536,128]{1,0:T(8,128)S(1)} custom-call(s32[1536]{0:T(1024)S(1)} %copy-done.10, f32[1536,128]{1,0:T(8,128)S(1)} %get-tuple-element.131.x.dsw, bf16[1536,3072]{1,0:T(8,128)(2,1)S(1)} %halves.1.b2), custom_call_target="tpu_custom_call" | custom-call | flops 1811939328 | bytes 11010048 | tf_op jit(solution)/shard_map/operator/pallas_call | solution.py:33
  183.7 2.0 stage2.1
  185.7 15.0 %all_to_all.23.x = f32[32,8,128]{2,1,0:T(8,128)S(1)} all-to-all(f32[32,8,128]{2,1,0:T(8,128)S(1)} %get-tuple-element.136), channel_id=1, replica_groups=mesh['cluster'=8,'sub'=32] {'sub'}, dimensions={0} | all-to-all | bytes 262144 | tf_op jit(solution)/shard_map/all_to_all | solution.py:606
  201.6 2.0 collective-permute-start.27
  203.6 1.4 collective-permute-start.28
  205.9 1.0 collective-permute-start.31
  206.9 1.8 collective-permute-start.30
  208.7 1.3 collective-permute-start.29
  210.0 4.9 %home.1 = (f32[1536,128]{1,0:T(8,128)S(1)}, f32[1536,128]{1,0:T(8,128)S(1)}, f32[1536,128]{1,0:T(8,128)S(1)}, f32[1536,128]{1,0:T(8,128)S(1)}, f32[1536,128]{1,0:T(8,128)S(1)}) custom-call(s32[1536]{0:T(1024)S(1)} %copy-done.10, f32[8,128]{1,0:T(8,128)S(1)} %get-tuple-element.143.scal2, f32[1536,128]{1,0:T(8,128)S(1)} %get-tuple-element.144.z2, ...), custom_call_target="tpu_custom_call" | custom-call | bytes 7868416 | tf_op jit(solution)/shard_map/home/pallas_call | solution.py:33
  214.9 2.7 %home_jump.1.s2 = f32[1536,128]{1,0:T(8,128)S(1)} custom-call(s32[8]{0:T(128)S(1)} %copy-done.13, s32[4]{0:T(128)S(1)} %bitcast.26, s32[1536]{0:T(1024)S(1)} %copy-done.10, f32[384,128]{1,0:T(8,128)S(1)} %get-tuple-element.153.ua, f32[384,128]{1,0:T(8,128)S(1)} %get-tuple-element.154.ub, f32[384,128]{1,0:T(8,128)S(1)} %get-tuple-element.155.uc, ...), custom_call_target="tpu_custom_call" | custom-call | bytes 2359296 | tf_op jit(solution)/shard_map/home_jump/pallas_call | solution.py:33
  217.6 1.4 last.1
  (86 shorter events, 13.9 us)
Async XLA Ops:
  8.2 20.2 %collective-permute-start.1 = (f32[768,128]{1,0:T(8,128)}, f32[768,128]{1,0:T(8,128)S(1)}, u32[]{:S(2)}, u32[]{:S(2)}) collective-permute-start(f32[768,128]{1,0:T(8,128)} %get-tuple-element.83.pb), channel_id=1, source_target_pairs={{1,2},{3,4},{5,6},{7,8},{9,10},{11,12},{13,14},{15,16},{17,18},{19... | collective-permute-start | bytes 1179656 | tf_op jit(solution)/shard_map/ppermute | solution.py:600
  8.9 19.5 %collective-permute-start.2 = (f32[768,128]{1,0:T(8,128)}, f32[768,128]{1,0:T(8,128)S(1)}, u32[]{:S(2)}, u32[]{:S(2)}) collective-permute-start(f32[768,128]{1,0:T(8,128)} %get-tuple-element.84.pc), channel_id=1, source_target_pairs={{0,32},{32,0},{64,96},{96,64},{128,160},{160,128},{192,224},{224,1... | collective-permute-start | bytes 1179656 | tf_op jit(solution)/shard_map/ppermute | solution.py:601
  9.0 19.4 %collective-permute-start.3 = (f32[768,128]{1,0:T(8,128)}, f32[768,128]{1,0:T(8,128)S(1)}, u32[]{:S(2)}, u32[]{:S(2)}) collective-permute-start(f32[768,128]{1,0:T(8,128)} %get-tuple-element.85.pd), channel_id=1, source_target_pairs={{32,64},{96,128},{160,192},{64,32},{128,96},{192,160},{33,65},{97,... | collective-permute-start | bytes 1179656 | tf_op jit(solution)/shard_map/ppermute | solution.py:602
  13.2 15.2 %collective-permute-start = (f32[768,128]{1,0:T(8,128)}, f32[768,128]{1,0:T(8,128)S(1)}, u32[]{:S(2)}, u32[]{:S(2)}) collective-permute-start(f32[768,128]{1,0:T(8,128)} %get-tuple-element.82.pa), channel_id=1, source_target_pairs={{0,1},{1,0},{2,3},{3,2},{4,5},{5,4},{6,7},{7,6},{8,9},{9,8},{10,11... | collective-permute-start | bytes 1179656 | tf_op jit(solution)/shard_map/ppermute | solution.py:599
  15.7 1.0 copy-start.1
  16.8 1.0 copy-start.3
  17.8 1.0 copy-start.5
  18.8 1.0 copy-start.7
  21.8 3.7 %copy-start = (f32[1,1,1536,1536]{3,2,1,0:T(8,128)S(1)}, f32[1,1,1536,1536]{3,2,1,0:T(8,128)}, u32[]{:S(2)}) copy-start(f32[1,1,1536,1536]{3,2,1,0:T(8,128)} %param.10) | copy-start | bytes 28311556
  25.5 1.5 copy-start.9
  25.5 1.5 copy-start.15
  25.5 2.9 %copy-start.2 = (f32[768,128]{1,0:T(8,128)S(1)}, f32[768,128]{1,0:T(8,128)}, u32[]{:S(2)}) copy-start(f32[768,128]{1,0:T(8,128)} %get-tuple-element.82.pa) | copy-start | bytes 1179652
  25.5 2.9 %copy-start.4 = (f32[768,128]{1,0:T(8,128)S(1)}, f32[768,128]{1,0:T(8,128)}, u32[]{:S(2)}) copy-start(f32[768,128]{1,0:T(8,128)} %get-tuple-element.83.pb) | copy-start | bytes 1179652
  25.5 2.9 %copy-start.6 = (f32[768,128]{1,0:T(8,128)S(1)}, f32[768,128]{1,0:T(8,128)}, u32[]{:S(2)}) copy-start(f32[768,128]{1,0:T(8,128)} %get-tuple-element.84.pc) | copy-start | bytes 1179652
  25.5 2.9 %copy-start.8 = (f32[768,128]{1,0:T(8,128)S(1)}, f32[768,128]{1,0:T(8,128)}, u32[]{:S(2)}) copy-start(f32[768,128]{1,0:T(8,128)} %get-tuple-element.85.pd) | copy-start | bytes 1179652
  25.6 2.9 %copy-start.13 = (s32[8]{0:T(128)S(1)}, s32[8]{0:T(128)}, u32[]{:S(2)}) copy-start(s32[8]{0:T(128)} %stack.36.place) | copy-start | bytes 100
  25.6 2.9 %copy-start.14 = (f32[8,128]{1,0:T(8,128)S(1)}, f32[8,128]{1,0:T(8,128)}, u32[]{:S(2)}) copy-start(f32[8,128]{1,0:T(8,128)} %get-tuple-element.81.crow) | copy-start | bytes 12292
  25.6 2.9 %copy-start.17 = (s32[1,1,4]{2,1,0:T(1,128)S(1)}, s32[1,1,4]{2,1,0:T(1,128)}, u32[]{:S(2)}) copy-start(s32[1,1,4]{2,1,0:T(1,128)} %param.18) | copy-start | bytes 52
  25.6 32.2 %copy-start.11 = (f32[1,48,384]{2,1,0:T(8,128)S(1)}, f32[1,48,384]{2,1,0:T(8,128)}, u32[]{:S(2)}) copy-start(f32[1,48,384]{2,1,0:T(8,128)} %param.15) | copy-start | bytes 221188
  27.0 33.5 %copy-start.10 = (s32[1536]{0:T(1024)S(1)}, s32[1536]{0:T(1024)}, u32[]{:S(2)}) copy-start(s32[1536]{0:T(1024)} %pad_add_fusion.idx) | copy-start | bytes 18436
  59.1 9.0 %collective-permute-start.4 = (f32[80,128]{1,0:T(8,128)S(1)}, f32[80,128]{1,0:T(8,128)S(1)}, u32[]{:S(2)}, u32[]{:S(2)}) collective-permute-start(f32[80,128]{1,0:T(8,128)S(1)} %get-tuple-element.97.own), channel_id=1, source_target_pairs={{0,32},{32,0},{64,96},{96,64},{128,160},{160,128},{192,224},{224,1... | collective-permute-start | bytes 122888 | tf_op jit(solution)/shard_map/ppermute | solution.py:612
  68.6 12.0 %collective-permute-start.7 = (f32[104,128]{1,0:T(8,128)S(1)}, f32[104,128]{1,0:T(8,128)S(1)}, u32[]{:S(2)}, u32[]{:S(2)}) collective-permute-start(f32[104,128]{1,0:T(8,128)S(1)} %pair.3.p2), channel_id=1, source_target_pairs={{0,192},{32,224},{64,128},{96,160},{128,64},{160,96},{192,0},{224,... | collective-permute-start | bytes 159752 | tf_op jit(solution)/shard_map/ppermute | solution.py:620
  70.8 9.9 %collective-permute-start.6 = (f32[104,128]{1,0:T(8,128)S(1)}, f32[104,128]{1,0:T(8,128)S(1)}, u32[]{:S(2)}, u32[]{:S(2)}) collective-permute-start(f32[104,128]{1,0:T(8,128)S(1)} %pair.3.p2), channel_id=1, source_target_pairs={{0,128},{32,160},{64,192},{96,224},{128,0},{160,32},{192,64},{224,... | collective-permute-start | bytes 159752 | tf_op jit(solution)/shard_map/ppermute | solution.py:620
  70.8 9.9 %collective-permute-start.5 = (f32[104,128]{1,0:T(8,128)S(1)}, f32[104,128]{1,0:T(8,128)S(1)}, u32[]{:S(2)}, u32[]{:S(2)}) collective-permute-start(f32[104,128]{1,0:T(8,128)S(1)} %pair.3.p2), channel_id=1, source_target_pairs={{0,64},{32,96},{64,0},{96,32},{128,192},{160,224},{192,128},{224,1... | collective-permute-start | bytes 159752 | tf_op jit(solution)/shard_map/ppermute | solution.py:620
  82.1 7.0 %collective-permute-start.8 = (f32[384,128]{1,0:T(8,128)S(1)}, f32[384,128]{1,0:T(8,128)S(1)}, u32[]{:S(2)}, u32[]{:S(2)}) collective-permute-start(f32[384,128]{1,0:T(8,128)S(1)} %get-tuple-element.106.ua.u0a), channel_id=1, source_target_pairs={{0,1},{1,0},{2,3},{3,2},{4,5},{5,4},{6,7},{7,6},{8,9},{9,8},{10,11... | collective-permute-start | bytes 589832 | tf_op jit(solution)/shard_map/ppermute | solution.py:599
  83.9 5.3 %collective-permute-start.9 = (f32[384,128]{1,0:T(8,128)S(1)}, f32[384,128]{1,0:T(8,128)S(1)}, u32[]{:S(2)}, u32[]{:S(2)}) collective-permute-start(f32[384,128]{1,0:T(8,128)S(1)} %get-tuple-element.107.ub.u0b), channel_id=1, source_target_pairs={{1,2},{3,4},{5,6},{7,8},{9,10},{11,12},{13,14},{15,16},{17,18},{19... | collective-permute-start | bytes 589832 | tf_op jit(solution)/shard_map/ppermute | solution.py:600
  84.5 4.6 %collective-permute-start.10 = (f32[384,128]{1,0:T(8,128)S(1)}, f32[384,128]{1,0:T(8,128)S(1)}, u32[]{:S(2)}, u32[]{:S(2)}) collective-permute-start(f32[384,128]{1,0:T(8,128)S(1)} %get-tuple-element.108.uc.u0c), channel_id=1, source_target_pairs={{0,32},{32,0},{64,96},{96,64},{128,160},{160,128},{192,224},{224,1... | collective-permute-start | bytes 589832 | tf_op jit(solution)/shard_map/ppermute | solution.py:601
  84.6 7.0 %collective-permute-start.11 = (f32[384,128]{1,0:T(8,128)S(1)}, f32[384,128]{1,0:T(8,128)S(1)}, u32[]{:S(2)}, u32[]{:S(2)}) collective-permute-start(f32[384,128]{1,0:T(8,128)S(1)} %get-tuple-element.109.ud.u0d), channel_id=1, source_target_pairs={{32,64},{96,128},{160,192},{64,32},{128,96},{192,160},{33,65},{97,... | collective-permute-start | bytes 589832 | tf_op jit(solution)/shard_map/ppermute | solution.py:602
  118.7 1.3 collective-permute-start.12
  120.6 11.7 %collective-permute-start.15 = (f32[104,128]{1,0:T(8,128)S(1)}, f32[104,128]{1,0:T(8,128)S(1)}, u32[]{:S(2)}, u32[]{:S(2)}) collective-permute-start(f32[104,128]{1,0:T(8,128)S(1)} %pair.4.p2), channel_id=1, source_target_pairs={{0,192},{32,224},{64,128},{96,160},{128,64},{160,96},{192,0},{224,... | collective-permute-start | bytes 159752 | tf_op jit(solution)/shard_map/ppermute | solution.py:620
  122.0 10.3 %collective-permute-start.14 = (f32[104,128]{1,0:T(8,128)S(1)}, f32[104,128]{1,0:T(8,128)S(1)}, u32[]{:S(2)}, u32[]{:S(2)}) collective-permute-start(f32[104,128]{1,0:T(8,128)S(1)} %pair.4.p2), channel_id=1, source_target_pairs={{0,128},{32,160},{64,192},{96,224},{128,0},{160,32},{192,64},{224,... | collective-permute-start | bytes 159752 | tf_op jit(solution)/shard_map/ppermute | solution.py:620
  122.9 9.5 %collective-permute-start.13 = (f32[104,128]{1,0:T(8,128)S(1)}, f32[104,128]{1,0:T(8,128)S(1)}, u32[]{:S(2)}, u32[]{:S(2)}) collective-permute-start(f32[104,128]{1,0:T(8,128)S(1)} %pair.4.p2), channel_id=1, source_target_pairs={{0,64},{32,96},{64,0},{96,32},{128,192},{160,224},{192,128},{224,1... | collective-permute-start | bytes 159752 | tf_op jit(solution)/shard_map/ppermute | solution.py:620
  134.0 6.2 %collective-permute-start.16 = (f32[384,128]{1,0:T(8,128)S(1)}, f32[384,128]{1,0:T(8,128)S(1)}, u32[]{:S(2)}, u32[]{:S(2)}) collective-permute-start(f32[384,128]{1,0:T(8,128)S(1)} %get-tuple-element.120.ua.u1a), channel_id=1, source_target_pairs={{0,1},{1,0},{2,3},{3,2},{4,5},{5,4},{6,7},{7,6},{8,9},{9,8},{10,11... | collective-permute-start | bytes 589832 | tf_op jit(solution)/shard_map/ppermute | solution.py:599
  134.9 5.2 %collective-permute-start.17 = (f32[384,128]{1,0:T(8,128)S(1)}, f32[384,128]{1,0:T(8,128)S(1)}, u32[]{:S(2)}, u32[]{:S(2)}) collective-permute-start(f32[384,128]{1,0:T(8,128)S(1)} %get-tuple-element.121.ub.u1b), channel_id=1, source_target_pairs={{1,2},{3,4},{5,6},{7,8},{9,10},{11,12},{13,14},{15,16},{17,18},{19... | collective-permute-start | bytes 589832 | tf_op jit(solution)/shard_map/ppermute | solution.py:600
  135.6 4.6 %collective-permute-start.18 = (f32[384,128]{1,0:T(8,128)S(1)}, f32[384,128]{1,0:T(8,128)S(1)}, u32[]{:S(2)}, u32[]{:S(2)}) collective-permute-start(f32[384,128]{1,0:T(8,128)S(1)} %get-tuple-element.122.uc.u1c), channel_id=1, source_target_pairs={{0,32},{32,0},{64,96},{96,64},{128,160},{160,128},{192,224},{224,1... | collective-permute-start | bytes 589832 | tf_op jit(solution)/shard_map/ppermute | solution.py:601
  135.7 7.0 %collective-permute-start.19 = (f32[384,128]{1,0:T(8,128)S(1)}, f32[384,128]{1,0:T(8,128)S(1)}, u32[]{:S(2)}, u32[]{:S(2)}) collective-permute-start(f32[384,128]{1,0:T(8,128)S(1)} %get-tuple-element.123.ud.u1d), channel_id=1, source_target_pairs={{32,64},{96,128},{160,192},{64,32},{128,96},{192,160},{33,65},{97,... | collective-permute-start | bytes 589832 | tf_op jit(solution)/shard_map/ppermute | solution.py:602
  170.0 1.3 collective-permute-start.20
  171.9 11.7 %collective-permute-start.23 = (f32[104,128]{1,0:T(8,128)S(1)}, f32[104,128]{1,0:T(8,128)S(1)}, u32[]{:S(2)}, u32[]{:S(2)}) collective-permute-start(f32[104,128]{1,0:T(8,128)S(1)} %pair.5.p2), channel_id=1, source_target_pairs={{0,192},{32,224},{64,128},{96,160},{128,64},{160,96},{192,0},{224,... | collective-permute-start | bytes 159752 | tf_op jit(solution)/shard_map/ppermute | solution.py:620
  173.3 10.3 %collective-permute-start.22 = (f32[104,128]{1,0:T(8,128)S(1)}, f32[104,128]{1,0:T(8,128)S(1)}, u32[]{:S(2)}, u32[]{:S(2)}) collective-permute-start(f32[104,128]{1,0:T(8,128)S(1)} %pair.5.p2), channel_id=1, source_target_pairs={{0,128},{32,160},{64,192},{96,224},{128,0},{160,32},{192,64},{224,... | collective-permute-start | bytes 159752 | tf_op jit(solution)/shard_map/ppermute | solution.py:620
  173.3 10.3 %collective-permute-start.21 = (f32[104,128]{1,0:T(8,128)S(1)}, f32[104,128]{1,0:T(8,128)S(1)}, u32[]{:S(2)}, u32[]{:S(2)}) collective-permute-start(f32[104,128]{1,0:T(8,128)S(1)} %pair.5.p2), channel_id=1, source_target_pairs={{0,64},{32,96},{64,0},{96,32},{128,192},{160,224},{192,128},{224,1... | collective-permute-start | bytes 159752 | tf_op jit(solution)/shard_map/ppermute | solution.py:620
  200.7 6.2 %collective-permute-start.24 = (f32[384,128]{1,0:T(8,128)S(1)}, f32[384,128]{1,0:T(8,128)S(1)}, u32[]{:S(2)}, u32[]{:S(2)}) collective-permute-start(f32[384,128]{1,0:T(8,128)S(1)} %get-tuple-element.153.ua), channel_id=1, source_target_pairs={{0,1},{1,0},{2,3},{3,2},{4,5},{5,4},{6,7},{7,6},{8,9},{9,8},{10,11... | collective-permute-start | bytes 589832 | tf_op jit(solution)/shard_map/ppermute | solution.py:599
  200.8 7.8 %collective-permute-start.25 = (f32[384,128]{1,0:T(8,128)S(1)}, f32[384,128]{1,0:T(8,128)S(1)}, u32[]{:S(2)}, u32[]{:S(2)}) collective-permute-start(f32[384,128]{1,0:T(8,128)S(1)} %get-tuple-element.154.ub), channel_id=1, source_target_pairs={{1,2},{3,4},{5,6},{7,8},{9,10},{11,12},{13,14},{15,16},{17,18},{19... | collective-permute-start | bytes 589832 | tf_op jit(solution)/shard_map/ppermute | solution.py:600
  201.5 13.4 %collective-permute-start.26 = (f32[384,128]{1,0:T(8,128)S(1)}, f32[384,128]{1,0:T(8,128)S(1)}, u32[]{:S(2)}, u32[]{:S(2)}) collective-permute-start(f32[384,128]{1,0:T(8,128)S(1)} %get-tuple-element.155.uc), channel_id=1, source_target_pairs={{0,32},{32,0},{64,96},{96,64},{128,160},{160,128},{192,224},{224,1... | collective-permute-start | bytes 589832 | tf_op jit(solution)/shard_map/ppermute | solution.py:601
  201.6 13.3 %collective-permute-start.27 = (f32[384,128]{1,0:T(8,128)S(1)}, f32[384,128]{1,0:T(8,128)S(1)}, u32[]{:S(2)}, u32[]{:S(2)}) collective-permute-start(f32[384,128]{1,0:T(8,128)S(1)} %get-tuple-element.156.ud), channel_id=1, source_target_pairs={{32,64},{96,128},{160,192},{64,32},{128,96},{192,160},{33,65},{97,... | collective-permute-start | bytes 589832 | tf_op jit(solution)/shard_map/ppermute | solution.py:602
  203.6 2.2 %collective-permute-start.28 = (f32[8,128]{1,0:T(8,128)S(1)}, f32[8,128]{1,0:T(8,128)S(1)}, u32[]{:S(2)}, u32[]{:S(2)}) collective-permute-start(f32[8,128]{1,0:T(8,128)S(1)} %sum.1.x), channel_id=1, source_target_pairs={{0,32},{32,0},{64,96},{96,64},{128,160},{160,128},{192,224},{224,1... | collective-permute-start | bytes 12296 | tf_op jit(solution)/shard_map/ppermute | solution.py:735
  205.9 11.7 %collective-permute-start.31 = (f32[8,128]{1,0:T(8,128)S(1)}, f32[8,128]{1,0:T(8,128)S(1)}, u32[]{:S(2)}, u32[]{:S(2)}) collective-permute-start(f32[8,128]{1,0:T(8,128)S(1)} %add.34.d0), channel_id=1, source_target_pairs={{0,192},{32,224},{64,128},{96,160},{128,64},{160,96},{192,0},{224,... | collective-permute-start | bytes 12296 | tf_op jit(solution)/shard_map/ppermute | solution.py:737
  206.9 10.6 %collective-permute-start.30 = (f32[8,128]{1,0:T(8,128)S(1)}, f32[8,128]{1,0:T(8,128)S(1)}, u32[]{:S(2)}, u32[]{:S(2)}) collective-permute-start(f32[8,128]{1,0:T(8,128)S(1)} %add.34.d0), channel_id=1, source_target_pairs={{0,128},{32,160},{64,192},{96,224},{128,0},{160,32},{192,64},{224,... | collective-permute-start | bytes 12296 | tf_op jit(solution)/shard_map/ppermute | solution.py:737
  208.7 8.9 %collective-permute-start.29 = (f32[8,128]{1,0:T(8,128)S(1)}, f32[8,128]{1,0:T(8,128)S(1)}, u32[]{:S(2)}, u32[]{:S(2)}) collective-permute-start(f32[8,128]{1,0:T(8,128)S(1)} %add.34.d0), channel_id=1, source_target_pairs={{0,64},{32,96},{64,0},{96,32},{128,192},{160,224},{192,128},{224,1... | collective-permute-start | bytes 12296 | tf_op jit(solution)/shard_map/ppermute | solution.py:737
  (2 other events, 1.3 us)
